TPU v7x, 128 devices: a whole 4x4x4 slice. The times are simulated.
128 devices in a mesh: row: 8 (over y_lo, x), col: 16 (over z, y_hi, core).
Axes of the slice: x: 4, y: 4 (y_hi: 2, y_lo: 2; y = y_hi * 2 + y_lo), z: 4, core: 2. Of those that a mesh axis runs over, the one named last changes fastest.
Arguments:
- voltages: float32 [1, 2, 2, 16777216], P(None, None, None, ('row', 'col')), may hold values from -6 to 6
- chirp_phase: float32 [1, 128, 131072], P(None, ('row', 'col')), may hold values from -3.140625 to 3.140625
Outputs:
- dedispersed: float32 [1, 2, 2, 16777216], P(None, None, None, ('row', 'col'))
All inputs are finite; a program needn't handle non-finite values.
Results may differ from a plain program's by a relative error of at most 0.00014.
Values sent between devices are 32-bit elements; how exact they have to be, the bound alone decides.
A program may use at most 128 MiB of HBM per device.

v0:
```python
import math

import jax
import jax.numpy as jnp
from jax import lax
from jax.sharding import PartitionSpec as P

SEG_HI = 512
SEG_LO = 256


def phase_table(left_index, right_index, modulus, direction):
    wrapped = left_index * right_index % modulus
    angles = direction * 2.0 * math.pi / modulus * wrapped.astype(jnp.float32)
    return (jnp.cos(angles), jnp.sin(angles))


def dft_tables(length, direction):
    indices = jnp.arange(length, dtype=jnp.int32)
    return phase_table(indices[:, None], indices[None, :], length, direction)


def twist(real_part, imag_part, cos_table, sin_table):
    return (
        real_part * cos_table - imag_part * sin_table,
        real_part * sin_table + imag_part * cos_table,
    )


def transform(pattern, real_part, imag_part, tables):
    cos_table, sin_table = tables

    def product(left, right):
        return jnp.einsum(pattern, left, right, precision=lax.Precision.HIGHEST)

    return (
        product(real_part, cos_table) - product(imag_part, sin_table),
        product(real_part, sin_table) + product(imag_part, cos_table),
    )


def regroup(blocks):
    leading, pieces, payload = blocks.shape
    shaped = blocks.reshape(leading, 1, pieces, payload)
    moved = lax.all_to_all(shaped, ("row", "col"), split_axis=2, concat_axis=1, tiled=True)
    return moved.reshape(leading, pieces, payload)


def dedisperse(voltages, chirp_local):
    channels = voltages.shape[0]
    polarizations = voltages.shape[1]
    samples = voltages.shape[3]
    pieces = lax.axis_size(("row", "col"))
    per_peer = samples // pieces
    total_len = pieces * samples
    device = lax.axis_index(("row", "col"))
    series_count = channels * polarizations
    hi_len = SEG_HI
    lo_len = SEG_LO
    blocks = regroup(voltages.reshape(series_count * 2, pieces, per_peer))
    blocks = blocks.reshape(series_count, 2, pieces, per_peer)
    real_part, imag_part = transform(
        "spj,kp->skj", blocks[:, 0], blocks[:, 1], dft_tables(pieces, -1.0)
    )
    offsets = device * per_peer + jnp.arange(per_peer, dtype=jnp.int32)
    cos_table, sin_table = phase_table(
        jnp.arange(pieces, dtype=jnp.int32)[:, None], offsets[None, :], total_len, -1.0
    )
    real_part, imag_part = twist(real_part, imag_part, cos_table, sin_table)
    blocks = regroup(
        jnp.stack([real_part, imag_part], 1).reshape(series_count * 2, pieces, per_peer)
    )
    blocks = blocks.reshape(series_count, 2, hi_len, lo_len)
    real_part, imag_part = transform(
        "smb,km->skb", blocks[:, 0], blocks[:, 1], dft_tables(hi_len, -1.0)
    )
    inner = jnp.arange(hi_len, dtype=jnp.int32)[:, None]
    outer = jnp.arange(lo_len, dtype=jnp.int32)[None, :]
    cos_table, sin_table = phase_table(inner, outer, samples, -1.0)
    real_part, imag_part = twist(real_part, imag_part, cos_table, sin_table)
    real_part, imag_part = transform("skm,lm->slk", real_part, imag_part, dft_tables(lo_len, -1.0))
    chirp_angles = chirp_local.reshape(channels, 1, lo_len, hi_len)
    real_part = real_part.reshape(channels, polarizations, lo_len, hi_len)
    imag_part = imag_part.reshape(channels, polarizations, lo_len, hi_len)
    real_part, imag_part = twist(real_part, imag_part, jnp.cos(chirp_angles), jnp.sin(chirp_angles))
    real_part = real_part.reshape(series_count, lo_len, hi_len)
    imag_part = imag_part.reshape(series_count, lo_len, hi_len)
    real_part, imag_part = transform("sba,mb->sam", real_part, imag_part, dft_tables(lo_len, 1.0))
    cos_table, sin_table = phase_table(inner, outer, samples, 1.0)
    real_part, imag_part = twist(real_part, imag_part, cos_table, sin_table)
    real_part, imag_part = transform("sam,na->snm", real_part, imag_part, dft_tables(hi_len, 1.0))
    real_part = real_part.reshape(series_count, samples)
    imag_part = imag_part.reshape(series_count, samples)
    positions = jnp.arange(samples, dtype=jnp.int32)
    cos_table, sin_table = phase_table(positions, device, total_len, 1.0)
    real_part, imag_part = twist(real_part, imag_part, cos_table, sin_table)
    blocks = regroup(
        jnp.stack([real_part, imag_part], 1).reshape(series_count * 2, pieces, per_peer)
    )
    blocks = blocks.reshape(series_count, 2, pieces, per_peer)
    real_part, imag_part = transform(
        "skj,pk->spj", blocks[:, 0], blocks[:, 1], dft_tables(pieces, 1.0)
    )
    scale = 1.0 / total_len
    blocks = jnp.stack([real_part * scale, imag_part * scale], 1).reshape(
        series_count * 2, pieces, per_peer
    )
    blocks = regroup(blocks)
    return blocks.reshape(channels, polarizations, 2, samples)


def body(voltages, chirp_phase):
    return dedisperse(voltages, chirp_phase)


def solution(mesh):
    placed = (P(None, None, None, ("row", "col")), P(None, ("row", "col"), None))
    return jax.shard_map(
        body,
        mesh=mesh,
        in_specs=placed,
        out_specs=P(None, None, None, ("row", "col")),
        check_vma=False,
    )
```

profile of v0, /device:TPU:1, one launch (start us, length us, event | category | flops | bytes accessed | tf_op | source)
XLA Modules:
  0.0 271.8 jit_solution(801744874579946850)
XLA Ops:
  0.0 3.1 %reshape_reshape.24 = f32[4,1,128,1024]{3,2,0,1:T(8,128)S(1)} reshape(f32[1,2,2,131072]{3,2,1,0:T(2,128)} %param.2) | data formatting | bytes 4194304 | tf_op jit(solution)/shard_map/reshape;reshape | solution.py:44
  3.1 2.7 copy.69
  5.7 11.9 %all-to-all-start = ((f32[4,1,128,1024]{3,0,1,2:T(4,128)}), f32[4,1,128,1024]{3,0,1,2:T(4,128)S(1)}, u32[]{:S(2)}, u32[]{:S(2)}) async-start(f32[4,1,128,1024]{3,0,1,2:T(4,128)} %copy.69), calls=%async_computation | async-start | bytes 4194304 | tf_op jit(solution)/shard_map/all_to_all | solution.py:45
  17.6 0.0 copy-done.4
  17.7 18.0 %cosine_reduce_fusion = (f32[131072]{0:T(1024)S(1)}, f32[131072]{0:T(1024)}) fusion(f32[1,1,131072]{2,1,0:T(1,128)S(1)} %copy-done.4), kind=kLoop, calls=%fused_computation.97 | loop fusion | bytes 1572864 | tf_op jit(solution)/shard_map/cos | solution.py:85
  35.7 0.1 cos.81
  35.7 1.1 sin.79
  36.9 2.9 %fusion.85 = (f32[128,1024]{1,0:T(8,128)}, f32[128,1024]{1,0:T(8,128)}) fusion(s32[1024]{0:T(1024)S(1)} %iota_add_fusion), kind=kLoop, calls=%fused_computation.133 | loop fusion | flops 1835008 | bytes 1052672 | tf_op jit(solution)/shard_map/cos | solution.py:15
  39.8 7.9 %all-to-all-done = f32[4,1,128,1024]{3,0,1,2:T(4,128)S(1)} async-done(((f32[4,1,128,1024]{3,0,1,2:T(4,128)}), f32[4,1,128,1024]{3,0,1,2:T(4,128)S(1)}, u32[]{:S(2)}, u32[]{:S(2)}) %all-to-all-start) | async-done | bytes 2097184 | tf_op jit(solution)/shard_map/all_to_all | solution.py:45
  47.7 1.2 copy.70
  48.9 1.3 fusion.35
  50.2 1.3 fusion.36
  51.5 0.0 copy-start
  51.5 0.0 copy-start.1
  51.5 1.3 convolution_add_fusion.3
  52.8 0.0 copy-done
  52.8 0.0 copy-done.1
  52.8 1.6 subtract_bitcast_fusion
  54.4 0.2 pad_maximum_fusion
  54.7 0.2 copy.73
  54.9 2.7 copy.74
  57.6 6.7 %all-to-all-start.1 = ((f32[4,1,128,1024]{3,0,1,2:T(4,128)}), f32[4,1,128,1024]{3,0,1,2:T(4,128)}, u32[]{:S(2)}, u32[]{:S(2)}) async-start(f32[4,1,128,1024]{3,0,1,2:T(4,128)} %copy.74), calls=%async_computation.1 | async-start | bytes 4194304 | tf_op jit(solution)/shard_map/all_to_all | solution.py:45
  64.3 2.1 multiply_sine_fusion.7
  66.3 2.9 %multiply_sine_fusion.6 = (f32[512,256]{1,0:T(8,128)}, f32[512,256]{1,0:T(8,128)}) fusion(), kind=kLoop, calls=%fused_computation.113 | loop fusion | flops 1835008 | bytes 1048576 | tf_op jit(solution)/shard_map/sin | solution.py:15
  69.3 2.1 fusion.82
  71.3 22.6 %all-to-all-done.1 = f32[4,1,128,1024]{3,0,1,2:T(4,128)} async-done(((f32[4,1,128,1024]{3,0,1,2:T(4,128)}), f32[4,1,128,1024]{3,0,1,2:T(4,128)}, u32[]{:S(2)}, u32[]{:S(2)}) %all-to-all-start.1) | async-done | bytes 2097184 | tf_op jit(solution)/shard_map/all_to_all | solution.py:45
  93.9 4.1 %copy.75 = f32[4,1,128,1024]{3,2,0,1:T(8,128)} copy(f32[4,1,128,1024]{3,0,1,2:T(4,128)} %all-to-all-done.1) | data formatting | bytes 4194304 | tf_op jit(solution)/shard_map/all_to_all | solution.py:45
  98.1 3.0 %reshape_reshape.27 = f32[2,2,512,256]{3,2,1,0:T(8,128)} reshape(f32[4,1,128,1024]{3,2,0,1:T(8,128)} %copy.75) | data formatting | bytes 4194304 | tf_op jit(solution)/shard_map/reshape;reshape | solution.py:73
  101.1 0.0 copy-start.2
  101.1 7.1 %fusion.27 = f32[512,2,256]{2,0,1:T(8,128)S(1)} fusion(f32[2,2,512,256]{3,2,1,0:T(8,128)} %reshape_reshape.27), kind=kOutput, calls=%fused_computation.51 | convolution fusion | flops 1614282752 | bytes 2097152 | tf_op jit(solution)/shard_map/smb,km->skb/dot_general | solution.py:34
  108.2 5.7 %fusion.23 = f32[512,2,256]{2,0,1:T(8,128)S(1)} fusion(f32[2,2,512,256]{3,2,1,0:T(8,128)S(1)} %copy-done.2), kind=kOutput, calls=%fused_computation.47 | convolution fusion | flops 1614282752 | bytes 2097152 | tf_op jit(solution)/shard_map/smb,km->skb/dot_general | solution.py:34
  113.9 5.9 %convolution_subtract_fusion.2 = f32[512,2,256]{2,0,1:T(8,128)S(1)} fusion(f32[512,2,256]{2,0,1:T(8,128)S(1)} %fusion.27, f32[2,2,512,256]{3,2,1,0:T(8,128)S(1)} %copy-done.2), kind=kOutput, calls=%fused_computation.17 | convolution fusion | flops 1614544896 | bytes 3145728 | tf_op jit(solution)/shard_map/smb,km->skb/dot_general | solution.py:34
  119.9 5.7 %convolution_add_fusion.2 = f32[512,2,256]{2,0,1:T(8,128)S(1)} fusion(f32[512,2,256]{2,0,1:T(8,128)S(1)} %fusion.23, f32[2,2,512,256]{3,2,1,0:T(8,128)S(1)} %copy-done.2), kind=kOutput, calls=%fused_computation.16 | convolution fusion | flops 1614544896 | bytes 3145728 | tf_op jit(solution)/shard_map/smb,km->skb/dot_general | solution.py:34
  125.6 2.6 fusion.21
  128.1 2.2 fusion.19
  130.3 2.2 convolution_subtract_fusion.5
  132.5 2.1 convolution_add_fusion.5
  134.6 2.8 %fusion.15 = f32[2,512,256]{2,1,0:T(8,128)S(1)} fusion(f32[256,2,512]{2,0,1:T(8,128)S(1)} %convolution_add_fusion.5, f32[256,2,512]{2,0,1:T(8,128)S(1)} %convolution_subtract_fusion.5, f32[256,512]{1,0:T(8,128)S(1)} %sin.79, f32[256,512]{1,0:T(8,128)S(1)} %cos.81), kind=kOutput, calls=%fused_computation.39 | convolution fusion | flops 807010304 | bytes 4194304 | tf_op jit(solution)/shard_map/sba,mb->sam/dot_general | solution.py:34
  137.4 3.0 %fusion.13 = f32[2,512,256]{2,1,0:T(8,128)S(1)} fusion(f32[256,2,512]{2,0,1:T(8,128)S(1)} %convolution_add_fusion.5, f32[256,2,512]{2,0,1:T(8,128)S(1)} %convolution_subtract_fusion.5, f32[256,512]{1,0:T(8,128)S(1)} %sin.79, f32[256,512]{1,0:T(8,128)S(1)} %cos.81), kind=kOutput, calls=%fused_computation.37 | convolution fusion | flops 807010304 | bytes 4194304 | tf_op jit(solution)/shard_map/sba,mb->sam/dot_general | solution.py:34
  140.4 2.8 %convolution_subtract_fusion.4 = f32[2,512,256]{2,1,0:T(8,128)S(1)} fusion(f32[2,512,256]{2,1,0:T(8,128)S(1)} %fusion.15, f32[256,2,512]{2,0,1:T(8,128)S(1)} %convolution_add_fusion.5, f32[256,2,512]{2,0,1:T(8,128)S(1)} %convolution_subtract_fusion.5, f32[256,512]{1,0:T(8,128)S(1)} %sin.79, f32[256,512]{1,0:T(8,128)S(1)} %cos.81), kind=kOutput, calls=%fused_computation.21 | convolution fusion | flops 807272448 | bytes 5242880 | tf_op jit(solution)/shard_map/sba,mb->sam/dot_general | solution.py:34
  143.2 2.8 %convolution_add_fusion.4 = f32[2,512,256]{2,1,0:T(8,128)S(1)} fusion(f32[2,512,256]{2,1,0:T(8,128)S(1)} %fusion.13, f32[256,2,512]{2,0,1:T(8,128)S(1)} %convolution_add_fusion.5, f32[256,2,512]{2,0,1:T(8,128)S(1)} %convolution_subtract_fusion.5, f32[256,512]{1,0:T(8,128)S(1)} %sin.79, f32[256,512]{1,0:T(8,128)S(1)} %cos.81), kind=kOutput, calls=%fused_computation.20 | convolution fusion | flops 807272448 | bytes 5242880 | tf_op jit(solution)/shard_map/sba,mb->sam/dot_general | solution.py:34
  146.1 6.0 %fusion.30 = f32[512,2,256]{2,0,1:T(8,128)S(1)} fusion(f32[2,512,256]{2,1,0:T(8,128)S(1)} %convolution_add_fusion.4, f32[2,512,256]{2,1,0:T(8,128)S(1)} %convolution_subtract_fusion.4, f32[512,256]{1,0:T(8,128)S(1)} %copy-done.5, f32[512,256]{1,0:T(8,128)S(1)} %copy-done.6), kind=kOutput, calls=%fused_computation.54 | convolution fusion | flops 1615069184 | bytes 4194304 | tf_op jit(solution)/shard_map/sam,na->snm/dot_general | solution.py:34
  152.1 6.8 %fusion.8 = f32[512,2,256]{2,0,1:T(8,128)} fusion(f32[2,512,256]{2,1,0:T(8,128)S(1)} %convolution_add_fusion.4, f32[2,512,256]{2,1,0:T(8,128)S(1)} %convolution_subtract_fusion.4, f32[512,256]{1,0:T(8,128)S(1)} %copy-done.5, f32[512,256]{1,0:T(8,128)S(1)} %copy-done.6), kind=kOutput, calls=%fused_computation.32 | convolution fusion | flops 1615069184 | bytes 4194304 | tf_op jit(solution)/shard_map/sam,na->snm/dot_general | solution.py:34
  158.9 6.8 %fusion.5 = f32[2,512,256]{2,1,0:T(8,128)} fusion(f32[512,2,256]{2,0,1:T(8,128)S(1)} %fusion.30, f32[2,512,256]{2,1,0:T(8,128)S(1)} %convolution_add_fusion.4, f32[2,512,256]{2,1,0:T(8,128)S(1)} %convolution_subtract_fusion.4, f32[512,256]{1,0:T(8,128)S(1)} %copy-done.5, f32[512,256]{1,0:T(8,128)S(1)} %copy-done.6), kind=kOutput, calls=%fused_computation.15 | convolution fusion | flops 1615331328 | bytes 5242880 | tf_op jit(solution)/shard_map/sam,na->snm/dot_general | solution.py:34
  165.8 2.4 reshape.308
  168.1 8.6 %fusion.4 = f32[2,512,256]{2,1,0:T(8,128)} fusion(f32[512,2,256]{2,0,1:T(8,128)} %fusion.8, f32[2,512,256]{2,1,0:T(8,128)} %copy-done.3, f32[2,512,256]{2,1,0:T(8,128)S(1)} %convolution_subtract_fusion.4, f32[512,256]{1,0:T(8,128)} %get-tuple-element.17, f32[512,256]{1,0:T(8,128)} %get-tuple-element.18), kind=kOutput, calls=%fused_computation.13 | convolution fusion | flops 1615331328 | bytes 5242880 | tf_op jit(solution)/shard_map/sam,na->snm/dot_general | solution.py:34
  176.8 1.9 reshape.309
  178.7 1.1 multiply_subtract_fusion
  179.9 0.9 pad_maximum_fusion.1
  180.8 1.6 copy.82
  182.4 2.9 %reshape_reshape.28 = f32[4,1,128,1024]{3,2,0,1:T(8,128)} reshape(f32[2,2,131072]{2,1,0:T(2,128)S(1)} %copy.82) | data formatting | bytes 4194304 | tf_op jit(solution)/shard_map/reshape;reshape | solution.py:44
  185.3 2.9 %copy.83 = f32[4,1,128,1024]{3,0,1,2:T(4,128)S(1)} copy(f32[4,1,128,1024]{3,2,0,1:T(8,128)} %reshape_reshape.28) | data formatting | bytes 4194304 | tf_op jit(solution)/shard_map/reshape;reshape | solution.py:44
  188.3 35.5 %all_to_all.16 = f32[4,1,128,1024]{3,0,1,2:T(4,128)S(1)} all-to-all(f32[4,1,128,1024]{3,0,1,2:T(4,128)S(1)} %copy.83), channel_id=1, replica_groups=mesh['row'=8,'col'=16] {'row','col'}, dimensions={2} | all-to-all | bytes 4194304 | tf_op jit(solution)/shard_map/all_to_all | solution.py:45
  223.7 1.2 copy.84
  225.0 1.3 fusion.38
  226.3 1.3 fusion.37
  227.5 1.3 fusion.3
  228.9 1.3 fusion.1
  230.2 0.2 pad_maximum_fusion.2
  230.4 0.2 copy.87
  230.7 1.4 copy.88
  232.0 35.5 %all_to_all.17 = f32[4,1,128,1024]{3,0,1,2:T(4,128)S(1)} all-to-all(f32[4,1,128,1024]{3,0,1,2:T(4,128)S(1)} %copy.88), channel_id=1, replica_groups=mesh['row'=8,'col'=16] {'row','col'}, dimensions={2} | all-to-all | bytes 4194304 | tf_op jit(solution)/shard_map/all_to_all | solution.py:45
  267.6 1.2 copy.89
  268.8 2.8 %reshape_reshape.31 = f32[1,2,2,131072]{3,2,1,0:T(2,128)} reshape(f32[4,1,128,1024]{3,2,0,1:T(8,128)S(1)} %copy.89) | data formatting | bytes 4194304 | tf_op jit(solution)/shard_map/reshape;reshape | solution.py:109
  (9 shorter events, 0.0 us)
Async XLA Ops:
  5.7 11.9 %copy-start.4 = (f32[1,1,131072]{2,1,0:T(1,128)S(1)}, f32[1,1,131072]{2,1,0:T(1,128)}, u32[]{:S(2)}) copy-start(f32[1,1,131072]{2,1,0:T(1,128)} %param.3) | copy-start | bytes 1572868
  5.7 42.0 %all-to-all-start = ((f32[4,1,128,1024]{3,0,1,2:T(4,128)}), f32[4,1,128,1024]{3,0,1,2:T(4,128)S(1)}, u32[]{:S(2)}, u32[]{:S(2)}) async-start(f32[4,1,128,1024]{3,0,1,2:T(4,128)} %copy.69), calls=%async_computation | async-start | bytes 4194304 | tf_op jit(solution)/shard_map/all_to_all | solution.py:45
  51.5 1.3 copy-start
  51.5 1.3 copy-start.1
  57.6 36.3 %all-to-all-start.1 = ((f32[4,1,128,1024]{3,0,1,2:T(4,128)}), f32[4,1,128,1024]{3,0,1,2:T(4,128)}, u32[]{:S(2)}, u32[]{:S(2)}) async-start(f32[4,1,128,1024]{3,0,1,2:T(4,128)} %copy.74), calls=%async_computation.1 | async-start | bytes 4194304 | tf_op jit(solution)/shard_map/all_to_all | solution.py:45
  101.1 7.1 %copy-start.2 = (f32[2,2,512,256]{3,2,1,0:T(8,128)S(1)}, f32[2,2,512,256]{3,2,1,0:T(8,128)}, u32[]{:S(2)}) copy-start(f32[2,2,512,256]{3,2,1,0:T(8,128)} %reshape_reshape.27) | copy-start | bytes 6291460
  143.2 2.8 %copy-start.5 = (f32[512,256]{1,0:T(8,128)S(1)}, f32[512,256]{1,0:T(8,128)}, u32[]{:S(2)}) copy-start(f32[512,256]{1,0:T(8,128)} %get-tuple-element.17) | copy-start | bytes 1572868
  143.2 2.8 %copy-start.6 = (f32[512,256]{1,0:T(8,128)S(1)}, f32[512,256]{1,0:T(8,128)}, u32[]{:S(2)}) copy-start(f32[512,256]{1,0:T(8,128)} %get-tuple-element.18) | copy-start | bytes 1572868
  146.0 12.9 %copy-start.3 = (f32[2,512,256]{2,1,0:T(8,128)}, f32[2,512,256]{2,1,0:T(8,128)S(1)}, u32[]{:S(2)}) copy-start(f32[2,512,256]{2,1,0:T(8,128)S(1)} %convolution_add_fusion.4) | copy-start | bytes 3145732
where the time goes:
time: 275 us; the launch traced here: 272 us
  matrix products  83.8 us (30%)
  blocking collectives  71 us (26%)
  local copies, waits for them, and re-layouts  54.9 us (20%)
  waiting for transfers between devices  30.5 us (11%)
  starting transfers between devices  18.6 us (7%)
  other arithmetic  12.5 us (5%)
    dot_general x24, matrix products, product(): return jnp.einsum(pattern, left, right, precision=lax.Precision.HIGHEST)  83.8 us
    all_to_all x2, blocking collectives, regroup(): lax.all_to_all(shaped, ('row', 'col'), split_axis=2, concat_axis=1, tiled...  71 us
    all_to_all x2, waiting for transfers between devices, regroup(): lax.all_to_all(shaped, ('row', 'col'), split_axis=2, concat_axis=1, tiled...  30.5 us
    all_to_all x2, starting transfers between devices, regroup(): lax.all_to_all(shaped, ('row', 'col'), split_axis=2, concat_axis=1, tiled...  18.6 us
    cos x2, local copies, waits for them, and re-layouts, dedisperse(): jnp.cos(chirp_angles)  18.1 us
    another operation x6, local copies, waits for them, and re-layouts, regroup(): shaped = blocks.reshape(leading, 1, pieces, payload)  15.6 us
    all_to_all x4, local copies, waits for them, and re-layouts, regroup(): lax.all_to_all(shaped, ('row', 'col'), split_axis=2, concat_axis=1, tiled...  7.78 us
    sin x3, other arithmetic, phase_table(): return (jnp.cos(angles), jnp.sin(angles))  7.03 us
  transfers between devices with their start and end apart: 2, of which 2 were waited for; matrix products, arithmetic and copies ran while one was open for 11% of the time, Pallas kernels for 0%

commit v1 on v0

v1 whole, which is shorter than its diff:
```python
import itertools
import math

import jax
import jax.numpy as jnp
import ml_dtypes
import numpy as np
from jax import lax
from jax.experimental import pallas as pl
from jax.experimental.pallas import tpu as pltpu
from jax.sharding import PartitionSpec as P

MESH = pl.DeviceIdType.MESH
F32 = jnp.float32
BF16 = jnp.bfloat16
PIECES = 128
LANES = 128
BLOCKS = 8
SEG = PIECES * BLOCKS * LANES
TOTAL = PIECES * SEG
DEVICE_DIMS = (2, 4, 4, 2, 2)
TILE = (8, 128)
SIZES = {"x": 4, "y": 4, "z": 4, "c": 2}
ORDERS = (("xc", "yz"), ("yz", "xc"), ("xc", "yz"), ("yz", "xc"))
STREAMS = 4
EXCHANGES = 4


def unit_roots(index, modulus):
    angles = -2.0 * math.pi * (index % modulus) / modulus
    return np.cos(angles), np.sin(angles)


def three_pass(matrix, axis):
    high = matrix.astype(ml_dtypes.bfloat16)
    low = (matrix - high.astype(np.float64)).astype(ml_dtypes.bfloat16)
    return np.concatenate([high, high, low], axis)


def tables():
    idx = np.arange(128, dtype=np.int64)
    re, im = unit_roots(idx[:, None] * idx[None, :], 128)
    left = lambda r, i: np.block([[r, -i], [i, r]])
    right = lambda r, i: np.block([[r, i], [-i, r]])
    offsets = np.arange(BLOCKS * LANES, dtype=np.int64).reshape(BLOCKS, 1, LANES)
    grid = offsets * idx[None, :, None]
    kb = np.arange(BLOCKS, dtype=np.int64)
    small = kb[:, None] * idx[None, :]
    f32 = lambda pair, axis: np.stack(pair, axis).astype(np.float32)
    return {
        "roots": f32((re, im), 0),
        "shift": f32(unit_roots(idx[:, None] * idx[None, :], 16384), 0),
        "outer": f32(unit_roots(grid, TOTAL), 1),
        "inner": f32(unit_roots(grid, SEG), 1),
        "small": f32(unit_roots(small, BLOCKS * LANES), 1),
        "left_fwd": three_pass(left(re, im), 1),
        "left_inv": three_pass(left(re, -im) / SEG, 1),
        "right_fwd": three_pass(right(re, im), 0),
        "right_inv": three_pass(right(re, -im), 0),
    }


TABLES = tables()
NAMES = tuple(TABLES)


def split(value):
    high = value.astype(BF16)
    low = (value - high.astype(F32)).astype(BF16)
    return high, low


def left_product(matrix, real, imag):
    high, low = split(jnp.concatenate([real, imag], 0))
    out = jnp.dot(matrix, jnp.concatenate([high, low, high], 0), preferred_element_type=F32)
    return out[:128], out[128:]


def right_product(value, matrix):
    high, low = split(value)
    return jnp.dot(jnp.concatenate([high, low, high], 1), matrix, preferred_element_type=F32)


def times(real, imag, cos, sin):
    return real * cos - imag * sin, real * sin + imag * cos


def times_conj(real, imag, cos, sin):
    return real * cos + imag * sin, imag * cos - real * sin


def add(a, b):
    return a[0] + b[0], a[1] + b[1]


def sub(a, b):
    return a[0] - b[0], a[1] - b[1]


def quarter(a, sign):
    return (-a[1], a[0]) if sign > 0 else (a[1], -a[0])


def dft4(z, sign):
    e0, e1 = add(z[0], z[2]), sub(z[0], z[2])
    o0, o1 = add(z[1], z[3]), quarter(sub(z[1], z[3]), sign)
    return [add(e0, o0), add(e1, o1), sub(e0, o0), sub(e1, o1)]


def dft8(z, sign):
    even, odd = dft4(z[0::2], sign), dft4(z[1::2], sign)
    root = math.sqrt(0.5)
    q1 = quarter(odd[1], sign)
    q3 = quarter(odd[3], sign)
    odd = [
        odd[0],
        ((odd[1][0] + q1[0]) * root, (odd[1][1] + q1[1]) * root),
        quarter(odd[2], sign),
        ((q3[0] - odd[3][0]) * root, (q3[1] - odd[3][1]) * root),
    ]
    return [add(even[k], odd[k]) for k in range(4)] + [sub(even[k], odd[k]) for k in range(4)]


def sin_cos(angle):
    half = angle * 0.5
    sq = half * half
    sine = 0.0
    for power in (13, 11, 9, 7, 5, 3, 1):
        sine = sine * sq + (-1.0) ** (power // 2) / math.factorial(power)
    cosine = 0.0
    for power in (12, 10, 8, 6, 4, 2, 0):
        cosine = cosine * sq + (-1.0) ** (power // 2) / math.factorial(power)
    sine = sine * half
    return 2.0 * sine * cosine, 1.0 - 2.0 * sine * sine


def where_is(coord):
    every = slice(None)
    y = coord.get("y")
    return (
        every if y is None else y % 2,
        coord.get("x", every),
        coord.get("z", every),
        every if y is None else y // 2,
        coord.get("c", every),
    )


def device_at(coord):
    y = coord["y"]
    return ((y % 2) * 4 + coord["x"], coord["z"] * 4 + (y // 2) * 2 + coord["c"])


def slot(exchange, stage):
    return exchange * 3 + stage - 1


SLOTS = 3 * EXCHANGES - 2


def kernel(x_ref, chirp_ref, *refs):
    count = len(NAMES)
    table_refs, out_ref, refs = refs[:count], refs[count], refs[count + 1 :]
    held, refs = dict(zip(NAMES, refs[:count])), refs[count:]
    (bufs, chirp_in, response, work, lanes_work, dev_fwd, dev_inv, send_sem, recv_sem, load_sem) = refs

    row, col = lax.axis_index("row"), lax.axis_index("col")
    me = row * 16 + col
    here = {"x": row % 4, "y": row // 4 + 2 * (col // 2 % 2), "z": col // 4, "c": col % 2}

    loads = {}
    for i, (name, src) in enumerate(zip(NAMES + ("chirp",), table_refs + (chirp_ref,))):
        dst = chirp_in if name == "chirp" else held[name]
        loads[name] = pltpu.make_async_copy(src, dst, load_sem.at[i])

    def peers(axes):
        for steps in itertools.product(*[range(SIZES[a]) for a in axes]):
            there = dict(here)
            for axis, step in zip(axes, steps):
                there[axis] = (here[axis] + step) % SIZES[axis]
            yield any(steps), there

    barrier = pltpu.get_barrier_semaphore()
    greeted = [there for axes in ORDERS[0] for remote, there in peers(axes) if remote]
    for there in greeted:
        pl.semaphore_signal(barrier, inc=1, device_id=device_at(there), device_id_type=MESH)
    for name in ("roots", "shift", "chirp", "outer", "left_fwd", "inner", "small", "right_fwd", "right_inv", "left_inv"):
        loads[name].start()
    pl.semaphore_wait(barrier, len(greeted))

    def stage_ref(stream, exchange, stage):
        if exchange == 0 and stage == 0:
            return x_ref.at[stream // 2, stream % 2]
        if exchange == EXCHANGES - 1 and stage == 2:
            return out_ref.at[stream // 2, stream % 2]
        return bufs.at[stream, slot(exchange, stage)]

    def sub_ref(stream, exchange, stage, where):
        if exchange == 0 and stage == 0:
            return x_ref.at[(stream // 2,) + where + (stream % 2,)]
        if exchange == EXCHANGES - 1 and stage == 2:
            return out_ref.at[(stream // 2,) + where + (stream % 2,)]
        return bufs.at[(stream, slot(exchange, stage)) + where]

    def sem_index(exchange, phase):
        return exchange * 2 + phase

    def send(stream, exchange, phase):
        axes = ORDERS[stream][phase]
        k = sem_index(exchange, phase)
        mine = where_is({a: here[a] for a in axes})
        for remote, there in peers(axes):
            src = sub_ref(stream, exchange, phase, where_is({a: there[a] for a in axes}))
            dst = sub_ref(stream, exchange, phase + 1, mine)
            if remote:
                pltpu.make_async_remote_copy(
                    src_ref=src,
                    dst_ref=dst,
                    send_sem=send_sem.at[stream, k],
                    recv_sem=recv_sem.at[stream, k],
                    device_id=device_at(there),
                    device_id_type=MESH,
                ).start()
            else:
                pltpu.make_async_copy(src, dst, recv_sem.at[stream, k]).start()

    def arrive(stream, exchange, phase):
        whole = sub_ref(stream, exchange, phase + 1, (slice(None),) * 5)
        pltpu.make_async_copy(whole, whole, recv_sem.at[stream, sem_index(exchange, phase)]).wait()

    def sent(stream, exchange, phase):
        share = math.prod(SIZES[a] for a in ORDERS[stream][phase])
        part = bufs.at[stream, 0].reshape(128, 8, 128).at[pl.ds(0, 128 - 128 // share)]
        pltpu.make_async_copy(part, part, send_sem.at[stream, sem_index(exchange, phase)]).wait()

    def flat(stream, exchange, stage):
        return bufs.at[stream, slot(exchange, stage)].reshape(1024, 128)

    def row_of(block, part):
        return pl.ds(block % 4 * 2 + part, 128, stride=8)

    def load_pair(refs2, block):
        out = []
        for part in range(2):
            out.append(
                jnp.concatenate([refs2[b // 4][row_of(b, part), :] for b in (block, block + 1)], 1)
            )
        return out

    def build_matrices():
        for name in ("roots", "shift"):
            loads[name].wait()
        re, im = held["roots"][0], held["roots"][1]
        sre, sim = held["shift"][0], held["shift"][1]
        on_lane = lax.broadcasted_iota(jnp.int32, (128, 128), 1) == me
        on_row = lax.broadcasted_iota(jnp.int32, (128, 128), 0) == me
        pick = lambda mask, v, axis: jnp.sum(jnp.where(mask, v, 0.0), axis=axis, keepdims=True)
        fre, fim = times(re, im, pick(on_lane, sre, 1), pick(on_lane, sim, 1))
        ire, iim = times(re, im, pick(on_row, sre, 0), pick(on_row, sim, 0))
        ire, iim = ire * (1.0 / PIECES), iim * (-1.0 / PIECES)
        for ref, r, i in ((dev_fwd, fre, fim), (dev_inv, ire, iim)):
            for half, (a, b) in enumerate(((r, -i), (i, r))):
                high, low = split(jnp.concatenate([a, b], 1))
                ref[pl.ds(half * 128, 128), :] = jnp.concatenate([high, high, low], 1)

    def build_response():
        loads["chirp"].wait()
        for kb in range(BLOCKS):
            angle = chirp_in[pl.ds(kb, 128, stride=8), :].T
            sine, cosine = sin_cos(angle)
            response[kb, 0] = cosine
            response[kb, 1] = sine

    def first_step(stream):
        src, dst = flat(stream, 0, 2), flat(stream, 1, 0)
        outer = held["outer"]
        for block in range(stream % 2 * 4, stream % 2 * 4 + 4, 2):
            real, imag = load_pair((src, src), block)
            real, imag = left_product(dev_fwd[...], real, imag)
            for i in range(2):
                b = block + i
                lanes = slice(i * 128, i * 128 + 128)
                r, m = times(real[:, lanes], imag[:, lanes], outer[b, 0], outer[b, 1])
                dst[row_of(b, 0), :] = r
                dst[row_of(b, 1), :] = m

    def middle_step(pol):
        src = [flat(2 * pol + h, 1, 2) for h in range(2)]
        dst = [flat(2 * pol + h, 2, 0) for h in range(2)]
        inner, small = held["inner"], held["small"]
        for block in range(0, BLOCKS, 2):
            real, imag = load_pair(src, block)
            real, imag = left_product(held["left_fwd"][...], real, imag)
            for i in range(2):
                b = block + i
                lanes = slice(i * 128, i * 128 + 128)
                r, m = times(real[:, lanes], imag[:, lanes], inner[b, 0], inner[b, 1])
                work[b, 0] = r
                work[b, 1] = m

        def forward(step, _):
            rows = pl.ds(pl.multiple_of(step * 8, 8), 8)
            z = dft8([(work[b, 0, rows, :], work[b, 1, rows, :]) for b in range(BLOCKS)], -1)
            for k in range(BLOCKS):
                r, m = z[k]
                if k:
                    r, m = times(r, m, small[k, 0:1, :], small[k, 1:2, :])
                lanes_work[k, rows, 0:128] = r
                lanes_work[k, rows, 128:256] = m
            return 0

        lax.fori_loop(0, 16, forward, 0)

        def across(step, _):
            ks = pl.ds(step * 2, 2)
            value = lanes_work[ks].reshape(256, 256)
            value = right_product(value, held["right_fwd"][...])
            ch = response[ks]
            cosine = ch[:, 0].reshape(256, 128)
            sine = ch[:, 1].reshape(256, 128)
            r, m = times(value[:, :128], value[:, 128:], cosine, sine)
            value = right_product(jnp.concatenate([r, m], 1), held["right_inv"][...])
            lanes_work[ks] = value.reshape(2, 128, 256)
            return 0

        lax.fori_loop(0, BLOCKS // 2, across, 0)

        def backward(step, _):
            rows = pl.ds(pl.multiple_of(step * 8, 8), 8)
            z = []
            for k in range(BLOCKS):
                r, m = lanes_work[k, rows, 0:128], lanes_work[k, rows, 128:256]
                if k:
                    r, m = times_conj(r, m, small[k, 0:1, :], small[k, 1:2, :])
                z.append((r, m))
            z = dft8(z, 1)
            for b in range(BLOCKS):
                r, m = times_conj(z[b][0], z[b][1], inner[b, 0, rows, :], inner[b, 1, rows, :])
                work[b, 0, rows, :] = r
                work[b, 1, rows, :] = m
            return 0

        lax.fori_loop(0, 16, backward, 0)

        for block in range(0, BLOCKS, 2):
            real = jnp.concatenate([work[block, 0], work[block + 1, 0]], 1)
            imag = jnp.concatenate([work[block, 1], work[block + 1, 1]], 1)
            real, imag = left_product(held["left_inv"][...], real, imag)
            for i in range(2):
                b = block + i
                lanes = slice(i * 128, i * 128 + 128)
                dst[b // 4][row_of(b, 0), :] = real[:, lanes]
                dst[b // 4][row_of(b, 1), :] = imag[:, lanes]

    def last_step(stream):
        src, dst = flat(stream, 2, 2), flat(stream, 3, 0)
        outer = held["outer"]
        for block in range(stream % 2 * 4, stream % 2 * 4 + 4, 2):
            parts = []
            for b in (block, block + 1):
                parts.append(times_conj(src[row_of(b, 0), :], src[row_of(b, 1), :], outer[b, 0], outer[b, 1]))
            real = jnp.concatenate([p[0] for p in parts], 1)
            imag = jnp.concatenate([p[1] for p in parts], 1)
            real, imag = left_product(dev_inv[...], real, imag)
            for i in range(2):
                b = block + i
                lanes = slice(i * 128, i * 128 + 128)
                dst[row_of(b, 0), :] = real[:, lanes]
                dst[row_of(b, 1), :] = imag[:, lanes]

    for stream in range(STREAMS):
        send(stream, 0, 0)
    build_matrices()
    for exchange in range(EXCHANGES):
        for pair in range(2):
            for stream in (2 * pair, 2 * pair + 1):
                arrive(stream, exchange, 0)
                send(stream, exchange, 1)
        if exchange == 0:
            build_response()
            for name in ("outer", "left_fwd", "inner", "small", "right_fwd", "right_inv", "left_inv"):
                loads[name].wait()
        for pair in range(2):
            streams = (2 * pair, 2 * pair + 1)
            if exchange == 1:
                for stream in streams:
                    arrive(stream, exchange, 1)
                middle_step(pair)
                for stream in streams:
                    send(stream, exchange + 1, 0)
                continue
            for stream in streams:
                arrive(stream, exchange, 1)
                if exchange == 0:
                    first_step(stream)
                if exchange == 2:
                    last_step(stream)
                if exchange < EXCHANGES - 1:
                    send(stream, exchange + 1, 0)
    for exchange in range(EXCHANGES):
        for phase in range(2):
            for stream in range(STREAMS):
                sent(stream, exchange, phase)


def body(voltages, chirp_phase):
    shape = (2,) + DEVICE_DIMS + (2,) + TILE
    rows = voltages.reshape(2, 2, PIECES * BLOCKS, LANES).transpose(0, 2, 1, 3).reshape(shape)
    any_space = pl.BlockSpec(memory_space=pl.ANY)
    values = [jnp.asarray(TABLES[name]) for name in NAMES]
    held = [pltpu.VMEM(v.shape, v.dtype) for v in values]
    out = pl.pallas_call(
        kernel,
        out_shape=jax.ShapeDtypeStruct(shape, F32),
        in_specs=[any_space] * (2 + len(values)),
        out_specs=any_space,
        scratch_shapes=held
        + [
            pltpu.VMEM((STREAMS, SLOTS) + DEVICE_DIMS + TILE, F32),
            pltpu.VMEM((PIECES * BLOCKS, LANES), F32),
            pltpu.VMEM((BLOCKS, 2, 128, 128), F32),
            pltpu.VMEM((BLOCKS, 2, 128, 128), F32),
            pltpu.VMEM((BLOCKS, 128, 256), F32),
            pltpu.VMEM((256, 768), BF16),
            pltpu.VMEM((256, 768), BF16),
            pltpu.SemaphoreType.DMA((STREAMS, 2 * EXCHANGES)),
            pltpu.SemaphoreType.DMA((STREAMS, 2 * EXCHANGES)),
            pltpu.SemaphoreType.DMA((len(values) + 1,)),
        ],
        name="dedisperse",
        compiler_params=pltpu.CompilerParams(
            collective_id=0, has_side_effects=True, vmem_limit_bytes=56 * 1024 * 1024
        ),
        cost_estimate=pl.CostEstimate(flops=5_000_000_000, bytes_accessed=9_000_000, transcendentals=0),
    )(rows, chirp_phase.reshape(PIECES * BLOCKS, LANES), *values)
    return out.reshape(2, PIECES * BLOCKS, 2, LANES).transpose(0, 2, 1, 3).reshape(voltages.shape)


def solution(mesh):
    placed = (P(None, None, None, ("row", "col")), P(None, ("row", "col"), None))
    return jax.shard_map(
        body,
        mesh=mesh,
        in_specs=placed,
        out_specs=P(None, None, None, ("row", "col")),
        check_vma=False,
    )
```

time: 275 us -> 110 us (0.40)
  Pallas kernels: 0 us -> 106 us
  matrix products: 83.8 us -> 0 us
  blocking collectives: 71 us -> 0 us
  local copies, waits for them, and re-layouts: 54.9 us -> 3.05 us
  waiting for transfers between devices: 30.5 us -> 0 us
  starting transfers between devices: 18.6 us -> 0 us
  other arithmetic: 12.5 us -> 0 us
    pallas_call x0 -> x1, Pallas kernels: none -> 106 us  [body(): pl.pallas_call(kernel, out_shape=jax.ShapeDtypeStruct(shape, F32), in_spe...]
    dot_general x24 -> x0, matrix products: 83.8 us -> none  [product(): return jnp.einsum(pattern, left, right, precision=lax.Precision.HIGHEST)]
    all_to_all x2 -> x0, blocking collectives: 71 us -> none  [regroup(): lax.all_to_all(shaped, ('row', 'col'), split_axis=2, concat_axis=1, tiled...]
    all_to_all x2 -> x0, waiting for transfers between devices: 30.5 us -> none  [regroup(): lax.all_to_all(shaped, ('row', 'col'), split_axis=2, concat_axis=1, tiled...]
    another operation x11 -> x0, local copies, waits for them, and re-layouts: 23.5 us -> none  [the longest x6 15.6 us: regroup(): shaped = blocks.reshape(leading, 1, pieces, payload)]
    all_to_all x2 -> x0, starting transfers between devices: 18.6 us -> none  [regroup(): lax.all_to_all(shaped, ('row', 'col'), split_axis=2, concat_axis=1, tiled...]
    cos x2 -> x0, local copies, waits for them, and re-layouts: 18.1 us -> none  [dedisperse(): jnp.cos(chirp_angles)]
    all_to_all x4 -> x0, local copies, waits for them, and re-layouts: 7.78 us -> none  [regroup(): lax.all_to_all(shaped, ('row', 'col'), split_axis=2, concat_axis=1, tiled...]
  transfers between devices with their start and end apart: 2 -> 0, of which waited for: 2 -> 0; matrix products, arithmetic and copies ran while one was open for 11% -> 0% of each run, Pallas kernels for 0% -> 0%
where the time goes in v1:
time: 110 us; the launch traced here: 109 us
  Pallas kernels  106 us (96%)
  local copies, waits for them, and re-layouts  3.05 us (3%)
    pallas_call x1, Pallas kernels, body(): pl.pallas_call(kernel, out_shape=jax.ShapeDtypeStruct(shape, F32), in_spe...  106 us
    unnamed x1, local copies, waits for them, and re-layouts  3.05 us

profile of v1, /device:TPU:1, one launch (start us, length us, event | category | flops | bytes accessed | tf_op | source)
XLA Modules:
  0.0 109.4 jit_solution(1748527643054072483)
XLA Ops:
  0.0 106.3 %dedisperse.1 = f32[2,2,4,4,2,2,2,8,128]{8,7,6,5,4,3,2,1,0:T(8,128)} custom-call(f32[2,2,4,4,2,2,2,8,128]{8,7,6,5,4,3,2,1,0:T(8,128)} %bitcast.12, f32[1024,128]{1,0:T(8,128)} %bitcast.13, f32[2,128,128]{2,1,0:T(8,128)} %constant.18.clone.refs_0_, f32[2,128,128]{2,1,0:T(8,128)} %constant.19.clone.refs_1_, f32[8,2,128,128]{3,2,1,0:T(8,128)} %constant.20.clone.refs_2_, ...), custom_call_target="tpu_custom_call" | custom-call | flops 5000000000 | bytes 9000000 | tf_op jit(solution)/shard_map/dedisperse/pallas_call | solution.py:412
  106.4 3.0 %copy.15 = f32[1,2,2,131072]{3,2,1,0:T(2,128)} copy(f32[1,2,2,131072]{3,2,1,0:T(2,128)} %bitcast.11) | data formatting | bytes 4194304

commit v2 on v1

--- a/solution.py
+++ b/solution.py
@@ -24,6 +24,9 @@
 ORDERS = (("xc", "yz"), ("yz", "xc"), ("xc", "yz"), ("yz", "xc"))
 STREAMS = 4
 EXCHANGES = 4
+UNROLL_A = 1
+UNROLL_C = 1
+WIDE = 2
 
 
 def unit_roots(index, modulus):
@@ -284,12 +287,11 @@
                 dst[row_of(b, 0), :] = r
                 dst[row_of(b, 1), :] = m
 
-    def middle_step(pol):
-        src = [flat(2 * pol + h, 1, 2) for h in range(2)]
-        dst = [flat(2 * pol + h, 2, 0) for h in range(2)]
-        inner, small = held["inner"], held["small"]
-        for block in range(0, BLOCKS, 2):
-            real, imag = load_pair(src, block)
+    def middle_open(stream):
+        src = flat(stream, 1, 2)
+        inner = held["inner"]
+        for block in range(stream % 2 * 4, stream % 2 * 4 + 4, 2):
+            real, imag = load_pair((src, src), block)
             real, imag = left_product(held["left_fwd"][...], real, imag)
             for i in range(2):
                 b = block + i
@@ -297,6 +299,9 @@
                 r, m = times(real[:, lanes], imag[:, lanes], inner[b, 0], inner[b, 1])
                 work[b, 0] = r
                 work[b, 1] = m
+
+    def middle_core():
+        inner, small = held["inner"], held["small"]
 
         def forward(step, _):
             rows = pl.ds(pl.multiple_of(step * 8, 8), 8)
@@ -309,21 +314,21 @@
                 lanes_work[k, rows, 128:256] = m
             return 0
 
-        lax.fori_loop(0, 16, forward, 0)
+        lax.fori_loop(0, 16, forward, 0, unroll=UNROLL_A)
 
         def across(step, _):
-            ks = pl.ds(step * 2, 2)
-            value = lanes_work[ks].reshape(256, 256)
+            ks = pl.ds(step * WIDE, WIDE)
+            value = lanes_work[ks].reshape(WIDE * 128, 256)
             value = right_product(value, held["right_fwd"][...])
             ch = response[ks]
-            cosine = ch[:, 0].reshape(256, 128)
-            sine = ch[:, 1].reshape(256, 128)
+            cosine = ch[:, 0].reshape(WIDE * 128, 128)
+            sine = ch[:, 1].reshape(WIDE * 128, 128)
             r, m = times(value[:, :128], value[:, 128:], cosine, sine)
             value = right_product(jnp.concatenate([r, m], 1), held["right_inv"][...])
-            lanes_work[ks] = value.reshape(2, 128, 256)
+            lanes_work[ks] = value.reshape(WIDE, 128, 256)
             return 0
 
-        lax.fori_loop(0, BLOCKS // 2, across, 0)
+        lax.fori_loop(0, BLOCKS // WIDE, across, 0, unroll=UNROLL_C)
 
         def backward(step, _):
             rows = pl.ds(pl.multiple_of(step * 8, 8), 8)
@@ -340,17 +345,19 @@
                 work[b, 1, rows, :] = m
             return 0
 
-        lax.fori_loop(0, 16, backward, 0)
-
-        for block in range(0, BLOCKS, 2):
+        lax.fori_loop(0, 16, backward, 0, unroll=UNROLL_A)
+
+    def middle_close(stream):
+        dst = flat(stream, 2, 0)
+        for block in range(stream % 2 * 4, stream % 2 * 4 + 4, 2):
             real = jnp.concatenate([work[block, 0], work[block + 1, 0]], 1)
             imag = jnp.concatenate([work[block, 1], work[block + 1, 1]], 1)
             real, imag = left_product(held["left_inv"][...], real, imag)
             for i in range(2):
                 b = block + i
                 lanes = slice(i * 128, i * 128 + 128)
-                dst[b // 4][row_of(b, 0), :] = real[:, lanes]
-                dst[b // 4][row_of(b, 1), :] = imag[:, lanes]
+                dst[row_of(b, 0), :] = real[:, lanes]
+                dst[row_of(b, 1), :] = imag[:, lanes]
 
     def last_step(stream):
         src, dst = flat(stream, 2, 2), flat(stream, 3, 0)
@@ -368,39 +375,42 @@
                 dst[row_of(b, 0), :] = real[:, lanes]
                 dst[row_of(b, 1), :] = imag[:, lanes]
 
+    def settle(step):
+        if step >= 0:
+            for stream in range(STREAMS):
+                sent(stream, step // 2, step % 2)
+
     for stream in range(STREAMS):
         send(stream, 0, 0)
     build_matrices()
     for exchange in range(EXCHANGES):
-        for pair in range(2):
-            for stream in (2 * pair, 2 * pair + 1):
-                arrive(stream, exchange, 0)
-                send(stream, exchange, 1)
+        for stream in range(STREAMS):
+            arrive(stream, exchange, 0)
+            send(stream, exchange, 1)
         if exchange == 0:
             build_response()
             for name in ("outer", "left_fwd", "inner", "small", "right_fwd", "right_inv", "left_inv"):
                 loads[name].wait()
+        settle(2 * exchange - 1)
+        settle(2 * exchange)
         for pair in range(2):
             streams = (2 * pair, 2 * pair + 1)
-            if exchange == 1:
-                for stream in streams:
-                    arrive(stream, exchange, 1)
-                middle_step(pair)
-                for stream in streams:
-                    send(stream, exchange + 1, 0)
-                continue
             for stream in streams:
                 arrive(stream, exchange, 1)
                 if exchange == 0:
                     first_step(stream)
+                if exchange == 1:
+                    middle_open(stream)
                 if exchange == 2:
                     last_step(stream)
-                if exchange < EXCHANGES - 1:
+                if exchange in (0, 2):
                     send(stream, exchange + 1, 0)
-    for exchange in range(EXCHANGES):
-        for phase in range(2):
-            for stream in range(STREAMS):
-                sent(stream, exchange, phase)
+            if exchange == 1:
+                middle_core()
+                for stream in streams:
+                    middle_close(stream)
+                    send(stream, exchange + 1, 0)
+    settle(2 * EXCHANGES - 1)
 
 
 def body(voltages, chirp_phase):
@@ -408,12 +418,13 @@
     rows = voltages.reshape(2, 2, PIECES * BLOCKS, LANES).transpose(0, 2, 1, 3).reshape(shape)
     any_space = pl.BlockSpec(memory_space=pl.ANY)
     values = [jnp.asarray(TABLES[name]) for name in NAMES]
+    operands = [rows, chirp_phase.reshape(PIECES * BLOCKS, LANES)] + values
     held = [pltpu.VMEM(v.shape, v.dtype) for v in values]
     out = pl.pallas_call(
         kernel,
-        out_shape=jax.ShapeDtypeStruct(shape, F32),
+        out_shape=pltpu.VMEM(shape, F32),
         in_specs=[any_space] * (2 + len(values)),
-        out_specs=any_space,
+        out_specs=pl.BlockSpec(memory_space=pltpu.VMEM),
         scratch_shapes=held
         + [
             pltpu.VMEM((STREAMS, SLOTS) + DEVICE_DIMS + TILE, F32),
@@ -429,10 +440,10 @@
         ],
         name="dedisperse",
         compiler_params=pltpu.CompilerParams(
-            collective_id=0, has_side_effects=True, vmem_limit_bytes=56 * 1024 * 1024
+            collective_id=0, has_side_effects=True, vmem_limit_bytes=48 * 1024 * 1024
         ),
         cost_estimate=pl.CostEstimate(flops=5_000_000_000, bytes_accessed=9_000_000, transcendentals=0),
-    )(rows, chirp_phase.reshape(PIECES * BLOCKS, LANES), *values)
+    )(*[pltpu.with_memory_space_constraint(v, pltpu.HBM) for v in operands])
     return out.reshape(2, PIECES * BLOCKS, 2, LANES).transpose(0, 2, 1, 3).reshape(voltages.shape)
 
 

time: 110 us -> 107 us (0.973)
  local copies, waits for them, and re-layouts: 3.05 us -> 1.32 us
    unnamed x1, local copies, waits for them, and re-layouts: 3.05 us -> 1.32 us
where the time goes in v2:
time: 107 us
  Pallas kernels  105 us (98%)
  local copies, waits for them, and re-layouts  1.32 us (1%)
    pallas_call x1, Pallas kernels, body(): pl.pallas_call(kernel, out_shape=pltpu.VMEM(shape, F32), in_specs=[any_sp...  105 us

profile of v2, /device:TPU:1, one launch (start us, length us, event | category | flops | bytes accessed | tf_op | source)
XLA Modules:
  0.0 106.8 jit_solution(16390537348290984282)
XLA Ops:
  0.0 105.5 %dedisperse.1 = f32[2,2,4,4,2,2,2,8,128]{8,7,6,5,4,3,2,1,0:T(8,128)S(1)} custom-call(f32[2,2,4,4,2,2,2,8,128]{8,7,6,5,4,3,2,1,0:T(8,128)} %bitcast.12, f32[1024,128]{1,0:T(8,128)} %bitcast.13, f32[2,128,128]{2,1,0:T(8,128)} %constant.18.clone.refs_0_, f32[2,128,128]{2,1,0:T(8,128)} %constant.19.clone.refs_1_, f32[8,2,128,128]{3,2,1,0:T(8,128)} %constant.20.clone.refs_2_, ...), custom_call_target="tpu_custom_call" | custom-call | flops 5000000000 | bytes 9000000 | tf_op jit(solution)/shard_map/dedisperse/pallas_call | solution.py:423
  105.5 1.3 %copy.15 = f32[1,2,2,131072]{3,2,1,0:T(2,128)} copy(f32[1,2,2,131072]{3,2,1,0:T(2,128)S(1)} %bitcast.11) | data formatting | bytes 4194304

commit v3 on v2

--- a/solution.py
+++ b/solution.py
@@ -24,9 +24,7 @@
 ORDERS = (("xc", "yz"), ("yz", "xc"), ("xc", "yz"), ("yz", "xc"))
 STREAMS = 4
 EXCHANGES = 4
-UNROLL_A = 1
-UNROLL_C = 1
-WIDE = 2
+DEPTH = 16
 
 
 def unit_roots(index, modulus):
@@ -34,10 +32,10 @@
     return np.cos(angles), np.sin(angles)
 
 
-def three_pass(matrix, axis):
+def three_pass(matrix, axis, tall=False):
     high = matrix.astype(ml_dtypes.bfloat16)
     low = (matrix - high.astype(np.float64)).astype(ml_dtypes.bfloat16)
-    return np.concatenate([high, high, low], axis)
+    return np.concatenate([high, low] if axis == 0 and tall else [high, high, low], axis)
 
 
 def tables():
@@ -56,8 +54,8 @@
         "outer": f32(unit_roots(grid, TOTAL), 1),
         "inner": f32(unit_roots(grid, SEG), 1),
         "small": f32(unit_roots(small, BLOCKS * LANES), 1),
-        "left_fwd": three_pass(left(re, im), 1),
-        "left_inv": three_pass(left(re, -im) / SEG, 1),
+        "left_fwd": three_pass(left(re, im), 0, True),
+        "left_inv": three_pass(left(re, -im) / SEG, 0, True),
         "right_fwd": three_pass(right(re, im), 0),
         "right_inv": three_pass(right(re, -im), 0),
     }
@@ -75,7 +73,8 @@
 
 def left_product(matrix, real, imag):
     high, low = split(jnp.concatenate([real, imag], 0))
-    out = jnp.dot(matrix, jnp.concatenate([high, low, high], 0), preferred_element_type=F32)
+    both = jnp.dot(matrix[:512], high, preferred_element_type=F32)
+    out = both[:256] + (both[256:] + jnp.dot(matrix[:256], low, preferred_element_type=F32))
     return out[:128], out[128:]
 
 
@@ -165,7 +164,7 @@
     count = len(NAMES)
     table_refs, out_ref, refs = refs[:count], refs[count], refs[count + 1 :]
     held, refs = dict(zip(NAMES, refs[:count])), refs[count:]
-    (bufs, chirp_in, response, work, lanes_work, dev_fwd, dev_inv, send_sem, recv_sem, load_sem) = refs
+    (bufs, chirp_in, response, work, dev_fwd, dev_inv, send_sem, recv_sem, load_sem) = refs
 
     row, col = lax.axis_index("row"), lax.axis_index("col")
     me = row * 16 + col
@@ -264,7 +263,8 @@
         for ref, r, i in ((dev_fwd, fre, fim), (dev_inv, ire, iim)):
             for half, (a, b) in enumerate(((r, -i), (i, r))):
                 high, low = split(jnp.concatenate([a, b], 1))
-                ref[pl.ds(half * 128, 128), :] = jnp.concatenate([high, high, low], 1)
+                ref[pl.ds(half * 128, 128), :] = high
+                ref[pl.ds(256 + half * 128, 128), :] = low
 
     def build_response():
         loads["chirp"].wait()
@@ -303,41 +303,24 @@
     def middle_core():
         inner, small = held["inner"], held["small"]
 
-        def forward(step, _):
-            rows = pl.ds(pl.multiple_of(step * 8, 8), 8)
+        def part(step, _):
+            rows = pl.ds(pl.multiple_of(step * DEPTH, DEPTH), DEPTH)
             z = dft8([(work[b, 0, rows, :], work[b, 1, rows, :]) for b in range(BLOCKS)], -1)
-            for k in range(BLOCKS):
-                r, m = z[k]
-                if k:
-                    r, m = times(r, m, small[k, 0:1, :], small[k, 1:2, :])
-                lanes_work[k, rows, 0:128] = r
-                lanes_work[k, rows, 128:256] = m
-            return 0
-
-        lax.fori_loop(0, 16, forward, 0, unroll=UNROLL_A)
-
-        def across(step, _):
-            ks = pl.ds(step * WIDE, WIDE)
-            value = lanes_work[ks].reshape(WIDE * 128, 256)
+            for k in range(1, BLOCKS):
+                z[k] = times(z[k][0], z[k][1], small[k, 0:1, :], small[k, 1:2, :])
+            value = jnp.concatenate([jnp.concatenate(pair, 1) for pair in z], 0)
             value = right_product(value, held["right_fwd"][...])
-            ch = response[ks]
-            cosine = ch[:, 0].reshape(WIDE * 128, 128)
-            sine = ch[:, 1].reshape(WIDE * 128, 128)
-            r, m = times(value[:, :128], value[:, 128:], cosine, sine)
-            value = right_product(jnp.concatenate([r, m], 1), held["right_inv"][...])
-            lanes_work[ks] = value.reshape(WIDE, 128, 256)
-            return 0
-
-        lax.fori_loop(0, BLOCKS // WIDE, across, 0, unroll=UNROLL_C)
-
-        def backward(step, _):
-            rows = pl.ds(pl.multiple_of(step * 8, 8), 8)
             z = []
             for k in range(BLOCKS):
-                r, m = lanes_work[k, rows, 0:128], lanes_work[k, rows, 128:256]
-                if k:
-                    r, m = times_conj(r, m, small[k, 0:1, :], small[k, 1:2, :])
-                z.append((r, m))
+                at = slice(k * DEPTH, k * DEPTH + DEPTH)
+                z.append(times(value[at, :128], value[at, 128:], response[k, 0, rows, :], response[k, 1, rows, :]))
+            value = jnp.concatenate([jnp.concatenate(pair, 1) for pair in z], 0)
+            value = right_product(value, held["right_inv"][...])
+            z = []
+            for k in range(BLOCKS):
+                at = slice(k * DEPTH, k * DEPTH + DEPTH)
+                r, m = value[at, :128], value[at, 128:]
+                z.append(times_conj(r, m, small[k, 0:1, :], small[k, 1:2, :]) if k else (r, m))
             z = dft8(z, 1)
             for b in range(BLOCKS):
                 r, m = times_conj(z[b][0], z[b][1], inner[b, 0, rows, :], inner[b, 1, rows, :])
@@ -345,7 +328,7 @@
                 work[b, 1, rows, :] = m
             return 0
 
-        lax.fori_loop(0, 16, backward, 0, unroll=UNROLL_A)
+        lax.fori_loop(0, 128 // DEPTH, part, 0, unroll=True)
 
     def middle_close(stream):
         dst = flat(stream, 2, 0)
@@ -431,9 +414,8 @@
             pltpu.VMEM((PIECES * BLOCKS, LANES), F32),
             pltpu.VMEM((BLOCKS, 2, 128, 128), F32),
             pltpu.VMEM((BLOCKS, 2, 128, 128), F32),
-            pltpu.VMEM((BLOCKS, 128, 256), F32),
-            pltpu.VMEM((256, 768), BF16),
-            pltpu.VMEM((256, 768), BF16),
+            pltpu.VMEM((512, 256), BF16),
+            pltpu.VMEM((512, 256), BF16),
             pltpu.SemaphoreType.DMA((STREAMS, 2 * EXCHANGES)),
             pltpu.SemaphoreType.DMA((STREAMS, 2 * EXCHANGES)),
             pltpu.SemaphoreType.DMA((len(values) + 1,)),

time: 107 us -> 105 us (0.981)
    pallas_call x1, Pallas kernels: 105 us -> 104 us  [body(): pl.pallas_call(kernel, out_shape=pltpu.VMEM(shape, F32), in_specs=[any_sp...]
where the time goes in v3:
time: 105 us
  Pallas kernels  104 us (99%)
  local copies, waits for them, and re-layouts  1.32 us (1%)
    pallas_call x1, Pallas kernels, body(): pl.pallas_call(kernel, out_shape=pltpu.VMEM(shape, F32), in_specs=[any_sp...  104 us

profile of v3, /device:TPU:1, one launch (start us, length us, event | category | flops | bytes accessed | tf_op | source)
XLA Modules:
  0.0 104.9 jit_solution(16982477229156304068)
XLA Ops:
  0.0 103.6 %dedisperse.1 = f32[2,2,4,4,2,2,2,8,128]{8,7,6,5,4,3,2,1,0:T(8,128)S(1)} custom-call(f32[2,2,4,4,2,2,2,8,128]{8,7,6,5,4,3,2,1,0:T(8,128)} %bitcast.12, f32[1024,128]{1,0:T(8,128)} %bitcast.13, f32[2,128,128]{2,1,0:T(8,128)} %constant.18.clone.refs_0_, f32[2,128,128]{2,1,0:T(8,128)} %constant.19.clone.refs_1_, f32[8,2,128,128]{3,2,1,0:T(8,128)} %constant.20.clone.refs_2_, ...), custom_call_target="tpu_custom_call" | custom-call | flops 5000000000 | bytes 9000000 | tf_op jit(solution)/shard_map/dedisperse/pallas_call | solution.py:406
  103.6 1.3 %copy.15 = f32[1,2,2,131072]{3,2,1,0:T(2,128)} copy(f32[1,2,2,131072]{3,2,1,0:T(2,128)S(1)} %bitcast.11) | data formatting | bytes 4194304

commit v4 on v3

--- a/solution.py
+++ b/solution.py
@@ -1,4 +1,3 @@
-import itertools
 import math
 
 import jax
@@ -23,6 +22,13 @@
 SIZES = {"x": 4, "y": 4, "z": 4, "c": 2}
 ORDERS = (("xc", "yz"), ("yz", "xc"), ("xc", "yz"), ("yz", "xc"))
 STREAMS = 4
+STEPS = {
+    "xc": ((1, 1), (3, 1), (2, 0), (2, 1), (1, 0), (3, 0), (0, 1), (0, 0)),
+    "yz": (
+        ((2, 2), (3, 2), (2, 1), (2, 3), (1, 2), (0, 2), (3, 1), (3, 3))
+        + ((2, 0), (1, 1), (1, 3), (0, 1), (0, 3), (3, 0), (1, 0), (0, 0))
+    ),
+}
 EXCHANGES = 4
 DEPTH = 16
 
@@ -175,8 +181,10 @@
         dst = chirp_in if name == "chirp" else held[name]
         loads[name] = pltpu.make_async_copy(src, dst, load_sem.at[i])
 
-    def peers(axes):
-        for steps in itertools.product(*[range(SIZES[a]) for a in axes]):
+    def peers(axes, mirror=False):
+        for steps in STEPS[axes]:
+            if mirror:
+                steps = tuple(-step % SIZES[axis] for axis, step in zip(axes, steps))
             there = dict(here)
             for axis, step in zip(axes, steps):
                 there[axis] = (here[axis] + step) % SIZES[axis]
@@ -211,7 +219,7 @@
         axes = ORDERS[stream][phase]
         k = sem_index(exchange, phase)
         mine = where_is({a: here[a] for a in axes})
-        for remote, there in peers(axes):
+        for remote, there in peers(axes, stream >= 2):
             src = sub_ref(stream, exchange, phase, where_is({a: there[a] for a in axes}))
             dst = sub_ref(stream, exchange, phase + 1, mine)
             if remote:
@@ -363,9 +371,11 @@
             for stream in range(STREAMS):
                 sent(stream, step // 2, step % 2)
 
-    for stream in range(STREAMS):
+    for stream in (0, 1):
         send(stream, 0, 0)
     build_matrices()
+    for stream in (2, 3):
+        send(stream, 0, 0)
     for exchange in range(EXCHANGES):
         for stream in range(STREAMS):
             arrive(stream, exchange, 0)

time: 105 us -> 104 us (level)
  Pallas kernels: 104 us -> 102 us
    pallas_call x1, Pallas kernels: 104 us -> 102 us  [body(): pl.pallas_call(kernel, out_shape=pltpu.VMEM(shape, F32), in_specs=[any_sp...]
where the time goes in v4:
time: 104 us
  Pallas kernels  102 us (98%)
  local copies, waits for them, and re-layouts  1.32 us (1%)
    pallas_call x1, Pallas kernels, body(): pl.pallas_call(kernel, out_shape=pltpu.VMEM(shape, F32), in_specs=[any_sp...  102 us

profile of v4, /device:TPU:1, one launch (start us, length us, event | category | flops | bytes accessed | tf_op | source)
XLA Modules:
  0.0 103.5 jit_solution(17694667984867031312)
XLA Ops:
  0.0 102.2 %dedisperse.1 = f32[2,2,4,4,2,2,2,8,128]{8,7,6,5,4,3,2,1,0:T(8,128)S(1)} custom-call(f32[2,2,4,4,2,2,2,8,128]{8,7,6,5,4,3,2,1,0:T(8,128)} %bitcast.12, f32[1024,128]{1,0:T(8,128)} %bitcast.13, f32[2,128,128]{2,1,0:T(8,128)} %constant.18.clone.refs_0_, f32[2,128,128]{2,1,0:T(8,128)} %constant.19.clone.refs_1_, f32[8,2,128,128]{3,2,1,0:T(8,128)} %constant.20.clone.refs_2_, ...), custom_call_target="tpu_custom_call" | custom-call | flops 5000000000 | bytes 9000000 | tf_op jit(solution)/shard_map/dedisperse/pallas_call | solution.py:416
  102.2 1.3 %copy.15 = f32[1,2,2,131072]{3,2,1,0:T(2,128)} copy(f32[1,2,2,131072]{3,2,1,0:T(2,128)S(1)} %bitcast.11) | data formatting | bytes 4194304

commit v5 on v4

--- a/solution.py
+++ b/solution.py
@@ -194,8 +194,6 @@
     greeted = [there for axes in ORDERS[0] for remote, there in peers(axes) if remote]
     for there in greeted:
         pl.semaphore_signal(barrier, inc=1, device_id=device_at(there), device_id_type=MESH)
-    for name in ("roots", "shift", "chirp", "outer", "left_fwd", "inner", "small", "right_fwd", "right_inv", "left_inv"):
-        loads[name].start()
     pl.semaphore_wait(barrier, len(greeted))
 
     def stage_ref(stream, exchange, stage):
@@ -373,6 +371,8 @@
 
     for stream in (0, 1):
         send(stream, 0, 0)
+    for name in ("roots", "shift", "chirp", "outer", "left_fwd", "inner", "small", "right_fwd", "right_inv", "left_inv"):
+        loads[name].start()
     build_matrices()
     for stream in (2, 3):
         send(stream, 0, 0)

time: 104 us -> 105 us (level)
    pallas_call x1, Pallas kernels: 102 us -> 103 us  [body(): pl.pallas_call(kernel, out_shape=pltpu.VMEM(shape, F32), in_specs=[any_sp...]
where the time goes in v5:
time: 105 us
  Pallas kernels  103 us (98%)
  local copies, waits for them, and re-layouts  1.32 us (1%)
    pallas_call x1, Pallas kernels, body(): pl.pallas_call(kernel, out_shape=pltpu.VMEM(shape, F32), in_specs=[any_sp...  103 us

profile of v5, /device:TPU:1, one launch (start us, length us, event | category | flops | bytes accessed | tf_op | source)
XLA Modules:
  0.0 104.8 jit_solution(10970518106632803457)
XLA Ops:
  0.0 103.5 %dedisperse.1 = f32[2,2,4,4,2,2,2,8,128]{8,7,6,5,4,3,2,1,0:T(8,128)S(1)} custom-call(f32[2,2,4,4,2,2,2,8,128]{8,7,6,5,4,3,2,1,0:T(8,128)} %bitcast.12, f32[1024,128]{1,0:T(8,128)} %bitcast.13, f32[2,128,128]{2,1,0:T(8,128)} %constant.18.clone.refs_0_, f32[2,128,128]{2,1,0:T(8,128)} %constant.19.clone.refs_1_, f32[8,2,128,128]{3,2,1,0:T(8,128)} %constant.20.clone.refs_2_, ...), custom_call_target="tpu_custom_call" | custom-call | flops 5000000000 | bytes 9000000 | tf_op jit(solution)/shard_map/dedisperse/pallas_call | solution.py:416
  103.5 1.3 %copy.15 = f32[1,2,2,131072]{3,2,1,0:T(2,128)} copy(f32[1,2,2,131072]{3,2,1,0:T(2,128)S(1)} %bitcast.11) | data formatting | bytes 4194304

commit v6 on v4

--- a/solution.py
+++ b/solution.py
@@ -384,8 +384,8 @@
             build_response()
             for name in ("outer", "left_fwd", "inner", "small", "right_fwd", "right_inv", "left_inv"):
                 loads[name].wait()
+        settle(2 * exchange - 2)
         settle(2 * exchange - 1)
-        settle(2 * exchange)
         for pair in range(2):
             streams = (2 * pair, 2 * pair + 1)
             for stream in streams:
@@ -403,6 +403,7 @@
                 for stream in streams:
                     middle_close(stream)
                     send(stream, exchange + 1, 0)
+    settle(2 * EXCHANGES - 2)
     settle(2 * EXCHANGES - 1)
 
 

time: 104 us -> 104 us (level)
  no operation moved by 1% of the time
where the time goes in v6:
time: 104 us
  Pallas kernels  102 us (98%)
  local copies, waits for them, and re-layouts  1.32 us (1%)
    pallas_call x1, Pallas kernels, body(): pl.pallas_call(kernel, out_shape=pltpu.VMEM(shape, F32), in_specs=[any_sp...  102 us

profile of v6, /device:TPU:1, one launch (start us, length us, event | category | flops | bytes accessed | tf_op | source)
XLA Modules:
  0.0 103.5 jit_solution(2269594313662869283)
XLA Ops:
  0.0 102.2 %dedisperse.1 = f32[2,2,4,4,2,2,2,8,128]{8,7,6,5,4,3,2,1,0:T(8,128)S(1)} custom-call(f32[2,2,4,4,2,2,2,8,128]{8,7,6,5,4,3,2,1,0:T(8,128)} %bitcast.12, f32[1024,128]{1,0:T(8,128)} %bitcast.13, f32[2,128,128]{2,1,0:T(8,128)} %constant.18.clone.refs_0_, f32[2,128,128]{2,1,0:T(8,128)} %constant.19.clone.refs_1_, f32[8,2,128,128]{3,2,1,0:T(8,128)} %constant.20.clone.refs_2_, ...), custom_call_target="tpu_custom_call" | custom-call | flops 5000000000 | bytes 9000000 | tf_op jit(solution)/shard_map/dedisperse/pallas_call | solution.py:417
  102.2 1.3 %copy.15 = f32[1,2,2,131072]{3,2,1,0:T(2,128)} copy(f32[1,2,2,131072]{3,2,1,0:T(2,128)S(1)} %bitcast.11) | data formatting | bytes 4194304
